TPU v7x, 32 devices: a whole 2x2x4 slice. The times are simulated.
32 devices in a mesh: tile: 8 (over z, x), head: 4 (over y, core).
Axes of the slice: x: 2, y: 2, z: 4, core: 2. Of those that a mesh axis runs over, the one named last changes fastest.
Arguments:
- tiles: bfloat16 [3072, 768], P('tile', 'head'), may hold values from -1 to 1
- first_norm_gain: float32 [768], replicated, may hold values from 0.5 to 1.5
- query_key_value_weight: bfloat16 [768, 3, 768], P(None, None, 'head'), may hold values from -1 to 1
- attention_out_weight: bfloat16 [768, 768], P('head'), may hold values from -0.21875 to 0.21875
- second_norm_gain: float32 [768], replicated, may hold values from 0.5 to 1.5
- first_feed_weight: bfloat16 [768, 3072], P(None, 'head'), may hold values from -0.21875 to 0.21875
- second_feed_weight: bfloat16 [3072, 768], P('head'), may hold values from -0.109375 to 0.109375
- slide_tile_counts: int32 [6], replicated, may hold values from 1 to 1536, 3072 in all
- dilation_head_offsets: int32 [12], P('head'), may hold values from 0 to 3
Outputs:
- layer_out: bfloat16 [3072, 768], P('tile', 'head')
Inputs may be any that keep to these rules, and one draw needn't show every extreme that they name: `slide_tile_counts`: the lengths sum to 3072; the longest is exactly 1536.
All inputs are finite; a program needn't handle non-finite values.
Results may differ from a plain program's by a relative error of at most 0.02.
Values may be sent and summed in bfloat16 or wider, within the bound.
A program may use at most 64 MiB of HBM per device.

v0:
```python
import jax
import jax.numpy as jnp
from jax import lax
from jax.sharding import PartitionSpec as P

HDIM = 64


def from_partner(array, axis, stride):
    return lax.ppermute(array, axis, [(i, i ^ 1 << stride) for i in range(lax.axis_size(axis))])


def layer_norm(values, gain):
    center = jnp.mean(values, axis=-1, keepdims=True)
    square = jnp.mean(values * values, axis=-1, keepdims=True)
    return (values - center) * lax.rsqrt(square - center * center + 1e-05) * gain


def take_half(values, chosen):
    shaped = values.reshape(values.shape[0], values.shape[1] // 2, 2, values.shape[2])
    return jnp.where((chosen == 0)[:, None, None], shaped[:, :, 0], shaped[:, :, 1])


def slide_number(positions, slide_ends):
    return jnp.sum((positions[..., None] >= slide_ends).astype(jnp.int32), axis=-1)


def spread_rows(values, stride_len):
    if values.ndim == 2:
        return jnp.broadcast_to(values[:, :, None], values.shape + (stride_len,)).reshape(
            values.shape[0], values.shape[1] * stride_len
        )
    wide = values.shape[:2] + (stride_len, values.shape[2])
    return jnp.broadcast_to(values[:, :, None, :], wide).reshape(
        values.shape[0], values.shape[1] * stride_len, values.shape[2]
    )


def sparse_dilated_attention(queries, key_value_pair, slide_tile_counts, offsets, tile_token_rows):
    slide_ends = jnp.cumsum(slide_tile_counts)[:-1]
    tile_place = lax.axis_index("tile")
    level_count = lax.axis_size("tile").bit_length() - 1
    row_index = jnp.arange(tile_token_rows, dtype=jnp.int32)
    keyed = key_value_pair
    own_rows = key_value_pair
    best = None
    denom = None
    accum = None
    for level_idx in range(level_count):
        stride_len = 2**level_idx
        sel_count = tile_token_rows // stride_len
        phase_off = offsets % stride_len
        if level_idx > 0:
            chosen = offsets >> level_idx - 1 & 1
            queries = take_half(queries, chosen)
            own_rows = take_half(keyed, chosen)
        partner = from_partner(own_rows, "tile", level_idx)
        upper_half = tile_place >> level_idx & 1 == 1
        keyed = jnp.where(
            upper_half,
            jnp.concatenate([partner, own_rows], axis=1),
            jnp.concatenate([own_rows, partner], axis=1),
        )
        group_start = (tile_place >> level_idx + 1 << level_idx + 1) * tile_token_rows
        key_slot = jnp.arange(keyed.shape[1], dtype=jnp.int32)
        key_posn = group_start + key_slot[None, :] * stride_len + phase_off[:, None]
        query_posn = (
            tile_place * tile_token_rows
            + jnp.arange(sel_count, dtype=jnp.int32)[None, :] * stride_len
            + phase_off[:, None]
        )
        same_slide = (
            slide_number(query_posn, slide_ends)[:, :, None]
            == slide_number(key_posn, slide_ends)[:, None, :]
        )
        scores = jnp.einsum(
            "hqd,hkd->hqk", queries, keyed[:, :, :HDIM], preferred_element_type=jnp.float32
        ) * HDIM ** (-0.5)
        scores = jnp.where(same_slide, scores, jnp.float32(-1e30))
        top_score = jnp.max(scores, axis=2)
        expo = jnp.exp(scores - top_score[:, :, None])
        sums = jnp.sum(expo, axis=2)
        weighted = jnp.einsum(
            "hqk,hkd->hqd",
            expo.astype(jnp.bfloat16),
            keyed[:, :, HDIM:],
            preferred_element_type=jnp.float32,
        )
        picked = row_index[None, :] % stride_len == phase_off[:, None]
        top_full = jnp.where(picked, spread_rows(top_score, stride_len), jnp.float32(-1e30))
        sum_full = jnp.where(picked, spread_rows(sums, stride_len), jnp.float32(0.0))
        acc_full = jnp.where(
            picked[:, :, None], spread_rows(weighted, stride_len), jnp.float32(0.0)
        )
        if level_idx == 0:
            best, denom, accum = (top_full, sum_full, acc_full)
        else:
            newest = jnp.maximum(best, top_full)
            old_weight = jnp.exp(best - newest)
            new_weight = jnp.exp(top_full - newest)
            denom = denom * old_weight + sum_full * new_weight
            accum = accum * old_weight[:, :, None] + acc_full * new_weight[:, :, None]
            best = newest
    return accum / denom[:, :, None]


def local(
    tiles,
    first_norm_gain,
    query_key_value_weight,
    attention_out_weight,
    second_norm_gain,
    first_feed_weight,
    second_feed_weight,
    slide_tile_counts,
    dilation_head_offsets,
):
    tile_token_rows = tiles.shape[0]
    feat_share = tiles.shape[1]
    resident_heads = dilation_head_offsets.shape[0]
    whole_tiles = lax.all_gather(tiles, "head", axis=1, tiled=True).astype(jnp.float32)
    ln1 = layer_norm(whole_tiles, first_norm_gain).astype(jnp.bfloat16)
    projected = jnp.einsum(
        "td,dcf->ctf", ln1, query_key_value_weight, preferred_element_type=jnp.float32
    ).astype(jnp.bfloat16)
    divide_into_heads = projected.reshape(3, tile_token_rows, resident_heads, HDIM).transpose(
        0, 2, 1, 3
    )
    key_value_pair = jnp.concatenate([divide_into_heads[1], divide_into_heads[2]], axis=-1)
    attended_rows = sparse_dilated_attention(
        divide_into_heads[0],
        key_value_pair,
        slide_tile_counts,
        dilation_head_offsets,
        tile_token_rows,
    )
    attn_flat = (
        attended_rows.astype(jnp.bfloat16).transpose(1, 0, 2).reshape(tile_token_rows, feat_share)
    )
    partial_out = jnp.dot(attn_flat, attention_out_weight, preferred_element_type=jnp.float32)
    summed = lax.psum_scatter(
        partial_out.astype(jnp.bfloat16), "head", scatter_dimension=1, tiled=True
    ).astype(jnp.float32)
    resid_own = (tiles.astype(jnp.float32) + summed).astype(jnp.bfloat16)
    resid_full = lax.all_gather(resid_own, "head", axis=1, tiled=True)
    ln2 = layer_norm(resid_full.astype(jnp.float32), second_norm_gain).astype(jnp.bfloat16)
    hidden = jax.nn.gelu(
        jnp.dot(ln2, first_feed_weight, preferred_element_type=jnp.float32)
    ).astype(jnp.bfloat16)
    mlp_out = lax.psum_scatter(
        jnp.dot(hidden, second_feed_weight, preferred_element_type=jnp.float32).astype(
            jnp.bfloat16
        ),
        "head",
        scatter_dimension=1,
        tiled=True,
    ).astype(jnp.float32)
    return (resid_own.astype(jnp.float32) + mlp_out).astype(jnp.bfloat16)


def solution(mesh):
    return jax.shard_map(
        local,
        mesh=mesh,
        in_specs=(
            P("tile", "head"),
            P(),
            P(None, None, "head"),
            P("head", None),
            P(),
            P(None, "head"),
            P("head", None),
            P(),
            P("head"),
        ),
        out_specs=P("tile", "head"),
        check_vma=False,
    )
```

profile of v0, /device:TPU:0, one launch (start us, length us, event | category | flops | bytes accessed | tf_op | source)
XLA Modules:
  0.0 130.5 jit_solution(6261574740723136185)
XLA Ops:
  6.5 9.3 %all_gather.6 = bf16[384,768]{0,1:T(8,128)(2,1)S(1)} all-gather(bf16[384,192]{0,1:T(8,128)(2,1)} %param.9), channel_id=1, replica_groups=mesh['tile'=8,'head'=4] {'head'}, dimensions={1}, use_global_device_ids=true | all-gather | bytes 737280 | tf_op jit(solution)/shard_map/all_gather | solution.py:121
  17.8 1.6 %collective-permute-start = (bf16[3,384,128]{1,2,0:T(8,128)(2,1)S(1)}, bf16[3,384,128]{1,2,0:T(8,128)(2,1)S(1)}, u32[]{:S(2)}, u32[]{:S(2)}) collective-permute-start(bf16[3,384,128]{1,2,0:T(8,128)(2,1)S(1)} %pad_maximum_fusion), channel_id=1, source_target_pairs={{0,4},{4,0},{8,12},{12,8},{16,20},{20,16},{24,28},{28,24},{1,5},{5... | collective-permute-start | bytes 884744 | tf_op jit(solution)/shard_map/ppermute | solution.py:10
  27.8 0.8 fusion.102
  30.6 1.6 %collective-permute-start.1 = (bf16[3,384,128]{1,2,0:T(8,128)(2,1)S(1)}, bf16[3,384,128]{1,2,0:T(8,128)(2,1)S(1)}, u32[]{:S(2)}, u32[]{:S(2)}) collective-permute-start(bf16[3,384,128]{1,2,0:T(8,128)(2,1)S(1)} %bitcast_select_fusion.1), channel_id=1, source_target_pairs={{0,8},{4,12},{8,0},{12,4},{16,24},{20,28},{24,16},{28,20},{1,9},{5... | collective-permute-start | bytes 884744 | tf_op jit(solution)/shard_map/ppermute | solution.py:10
  32.3 1.7 %fusion.2 = (f32[3,384]{1,0:T(4,128)S(1)}, f32[3,384,768]{2,1,0:T(8,128)S(1)}) fusion(s32[3,768]{1,0:T(4,128)S(1)} %copy-done.9, s32[3,384]{1,0:T(4,128)S(1)} %copy-done.16, bf16[3,768,128]{1,2,0:T(8,128)(2,1)S(1)} %maximum_select_fusion, bf16[3,3,384,64]{2,3,1,0:T(8,128)(2,1)} %bitcast.72), kind=kOutput, calls=%fused_computation.4 | convolution fusion | flops 116784000 | bytes 4004352 | tf_op jit(solution)/shard_map/hqd,hkd->hqk/dot_general | solution.py:76
  34.0 1.7 %fusion = f32[3,384]{1,0:T(4,128)} fusion(f32[3,384,768]{2,1,0:T(8,128)S(1)} %get-tuple-element.39, f32[3,384]{1,0:T(4,128)S(1)} %get-tuple-element.38, s32[3,768]{1,0:T(4,128)S(1)} %copy-done.9, s32[3,384]{1,0:T(4,128)S(1)} %copy-done.16), kind=kLoop, calls=%fused_computation.2 | loop fusion | flops 4422528 | bytes 3561984 | tf_op jit(solution)/shard_map/reduce_sum | solution.py:82
  35.8 3.9 %collective-permute-done.1 = bf16[3,384,128]{1,2,0:T(8,128)(2,1)S(1)} collective-permute-done((bf16[3,384,128]{1,2,0:T(8,128)(2,1)S(1)}, bf16[3,384,128]{1,2,0:T(8,128)(2,1)S(1)}, u32[]{:S(2)}, u32[]{:S(2)}) %collective-permute-start.1) | collective-permute-done | bytes 294944 | tf_op jit(solution)/shard_map/ppermute | solution.py:10
  42.7 2.6 %collective-permute-start.2 = (bf16[3,384,128]{1,2,0:T(8,128)(2,1)}, bf16[3,384,128]{1,2,0:T(8,128)(2,1)}, u32[]{:S(2)}, u32[]{:S(2)}) collective-permute-start(bf16[3,384,128]{1,2,0:T(8,128)(2,1)} %bitcast_select_fusion), channel_id=1, source_target_pairs={{0,16},{4,20},{8,24},{12,28},{16,0},{20,4},{24,8},{28,12},{1,17},{... | collective-permute-start | bytes 884744 | tf_op jit(solution)/shard_map/ppermute | solution.py:10
  45.3 1.6 %fusion.107 = (f32[3,192]{1,0:T(4,128)S(1)}, f32[3,192,768]{2,1,0:T(8,128)S(1)}) fusion(bf16[3,768,128]{1,2,0:T(8,128)(2,1)S(1)} %maximum_select_fusion.1, bf16[3,192,1,64]{1,3,2,0:T(8,128)(2,1)} %copy.70, bf16[3,192,1,64]{1,3,2,0:T(8,128)(2,1)} %copy.69, pred[3]{0:T(512)(128)(4,1)} %copy-done.27, s32[3,768]{1,0:T(4,128)} %get-tuple-element.9, ...), kind=kOutput, calls=%fused_computation.148 | convolution fusion | flops 58428864 | bytes 2225667 | tf_op jit(solution)/shard_map/hqd,hkd->hqk/dot_general | solution.py:76
  46.9 1.1 fusion.5
  48.0 0.9 broadcast_in_dim.91
  48.9 1.8 %reshape.689 = f32[3,384]{1,0:T(4,128)} reshape(f32[3,192,2]{2,1,0:T(8,128)} %broadcast_in_dim.91) | data formatting | bytes 9216 | tf_op jit(solution)/shard_map/reshape | solution.py:30
  50.7 1.6 %broadcast_in_dim.104 = f32[3,192,2]{2,1,0:T(8,128)} broadcast(f32[3,192]{1,0:T(4,128)} %fusion.5), dimensions={0,1} | broadcast | bytes 6912 | tf_op jit(solution)/shard_map/broadcast_in_dim | solution.py:30
  52.3 1.8 %reshape.693 = f32[3,384]{1,0:T(4,128)} reshape(f32[3,192,2]{2,1,0:T(8,128)} %broadcast_in_dim.104) | data formatting | bytes 9216 | tf_op jit(solution)/shard_map/reshape | solution.py:30
  55.0 3.4 %collective-permute-done.2 = bf16[3,384,128]{1,2,0:T(8,128)(2,1)} collective-permute-done((bf16[3,384,128]{1,2,0:T(8,128)(2,1)}, bf16[3,384,128]{1,2,0:T(8,128)(2,1)}, u32[]{:S(2)}, u32[]{:S(2)}) %collective-permute-start.2) | collective-permute-done | bytes 294944 | tf_op jit(solution)/shard_map/ppermute | solution.py:10
  58.4 1.4 %maximum_select_fusion.2 = bf16[3,768,128]{1,2,0:T(8,128)(2,1)S(1)} fusion(bf16[3,384,128]{1,2,0:T(8,128)(2,1)} %bitcast_select_fusion, bf16[3,384,128]{1,2,0:T(8,128)(2,1)} %collective-permute-done.2, pred[]{:T(512)S(6)} %eq.160), kind=kLoop, calls=%fused_computation.52 | loop fusion | flops 2654208 | bytes 1179649 | tf_op jit(solution)/shard_map/jit(_where)/select_n | solution.py:59
  62.2 3.2 %fusion.39 = bf16[3,384,64]{1,2,0:T(8,128)(2,1)S(1)} fusion(f32[3,384,768]{2,1,0:T(8,128)} %copy-done.1, f32[3,384]{1,0:T(4,128)S(1)} %copy-done.14, s32[3,768]{1,0:T(4,128)S(1)} %copy-done.10, s32[3,384]{1,0:T(4,128)S(1)} %copy-done.17, bf16[3,768,128]{1,2,0:T(8,128)(2,1)S(1)} %copy-done.3, f32[3,384,64]{1,2,0:T(8,128)S(1)} %copy.82, ...), kind=kOutput, calls=%fused_computation.42 | convolution fusion | flops 118407168 | bytes 4629504 | tf_op jit(solution)/shard_map/hqk,hkd->hqd/dot_general | solution.py:83
  65.4 1.2 convolution_convert_fusion.1
  66.7 22.0 %reduce-scatter.3.cloned.1.call-done = bf16[384,192]{0,1:T(8,128)(2,1)} async-done(((bf16[384,768]{0,1:T(8,128)(2,1)}), bf16[384,192]{0,1:T(8,128)(2,1)}) %reduce-scatter.3.cloned.1.call-update) | async-done | bytes 147472 | tf_op jit(solution)/shard_map/reduce_scatter | solution.py:141
  88.6 0.9 add_convert_fusion.1
  89.6 7.1 %all_gather.7 = bf16[384,768]{0,1:T(8,128)(2,1)S(1)} all-gather(bf16[384,192]{0,1:T(8,128)(2,1)S(1)} %add_convert_fusion.1), channel_id=1, replica_groups=mesh['tile'=8,'head'=4] {'head'}, dimensions={1}, use_global_device_ids=true | all-gather | bytes 737280 | tf_op jit(solution)/shard_map/all_gather | solution.py:145
  97.0 2.5 %convolution_convert_fusion = bf16[384,768]{0,1:T(8,128)(2,1)} fusion(bf16[768,768]{1,0:T(8,128)(2,1)S(1)} %copy-done, bf16[768,768]{1,0:T(8,128)(2,1)S(1)} %copy-done.28, bf16[384,768]{0,1:T(8,128)(2,1)S(1)} %all_gather.7, f32[768]{0:T(1024)S(1)} %copy-done.31, f32[384]{0:T(512)S(1)} %get-tuple-element.31, f32[384]{0:T(512)S(1)} %get-tuple-element.30), kind=kOutput, calls=%fused_computation.17 | convolution fusion | flops 910393344 | bytes 3545088 | tf_op jit(solution)/shard_map/dot_general | solution.py:151
  99.5 22.6 %reduce-scatter.5.cloned.1.call-done = bf16[384,192]{0,1:T(8,128)(2,1)} async-done(((bf16[384,768]{0,1:T(8,128)(2,1)}), bf16[384,192]{0,1:T(8,128)(2,1)}) %reduce-scatter.5.cloned.1.call-update) | async-done | bytes 147472 | tf_op jit(solution)/shard_map/reduce_scatter | solution.py:150
  122.1 1.6 %add_convert_fusion = bf16[384,192]{0,1:T(8,128)(2,1)} fusion(bf16[384,192]{0,1:T(8,128)(2,1)} %reduce-scatter.5.cloned.1.call-done, bf16[384,192]{0,1:T(8,128)(2,1)S(1)} %add_convert_fusion.1), kind=kLoop, calls=%fused_computation.75 | loop fusion | flops 294912 | bytes 442368 | tf_op jit(solution)/shard_map/convert_element_type | solution.py:158
  (133 shorter events, 18.6 us)
Async XLA Ops:
  6.5 90.4 %copy-start = (bf16[768,768]{1,0:T(8,128)(2,1)S(1)}, bf16[768,768]{1,0:T(8,128)(2,1)}, u32[]{:S(2)}) copy-start(bf16[768,768]{1,0:T(8,128)(2,1)} %param.15) | copy-start | bytes 3538948
  6.5 9.6 %copy-start.29 = (bf16[768,3,192]{0,2,1:T(8,128)(2,1)S(1)}, bf16[768,3,192]{0,2,1:T(8,128)(2,1)}, u32[]{:S(2)}) copy-start(bf16[768,3,192]{0,2,1:T(8,128)(2,1)} %param.11) | copy-start | bytes 2654212
  6.5 9.6 %copy-start.30 = (f32[768]{0:T(1024)S(1)}, f32[768]{0:T(1024)}, u32[]{:S(2)}) copy-start(f32[768]{0:T(1024)} %param.10) | copy-start | bytes 9220
  6.5 82.1 %reduce-scatter.3.cloned.1.call-start = ((), (), s32[]{:S(2)}) async-start(), calls=%async_computation.2 | async-start | bytes 737280 | tf_op jit(solution)/shard_map/reduce_scatter | solution.py:141
  16.8 2.5 %copy-start.32 = (s32[3]{0:T(128)S(1)}, s32[3]{0:T(128)}, u32[]{:S(2)}) copy-start(s32[3]{0:T(128)} %param.17) | copy-start | bytes 40
  17.8 9.6 %collective-permute-start = (bf16[3,384,128]{1,2,0:T(8,128)(2,1)S(1)}, bf16[3,384,128]{1,2,0:T(8,128)(2,1)S(1)}, u32[]{:S(2)}, u32[]{:S(2)}) collective-permute-start(bf16[3,384,128]{1,2,0:T(8,128)(2,1)S(1)} %pad_maximum_fusion), channel_id=1, source_target_pairs={{0,4},{4,0},{8,12},{12,8},{16,20},{20,16},{24,28},{28,24},{1,5},{5... | collective-permute-start | bytes 884744 | tf_op jit(solution)/shard_map/ppermute | solution.py:10
  19.3 5.3 %copy-start.27 = (pred[3]{0:T(512)(128)(4,1)}, pred[3]{0:T(512)(128)(4,1)S(1)}, u32[]{:S(2)}) copy-start(pred[3]{0:T(512)(128)(4,1)S(1)} %get-tuple-element.35) | copy-start | bytes 13
  19.4 22.6 %copy-start.25 = (pred[3]{0:T(512)(128)(4,1)}, pred[3]{0:T(512)(128)(4,1)S(1)}, u32[]{:S(2)}) copy-start(pred[3]{0:T(512)(128)(4,1)S(1)} %get-tuple-element.34) | copy-start | bytes 13
  19.4 7.2 %copy-start.21 = (s32[3]{0:T(128)}, s32[3]{0:T(128)S(1)}, u32[]{:S(2)}) copy-start(s32[3]{0:T(128)S(1)} %get-tuple-element.36) | copy-start | bytes 40
  19.4 7.2 %copy-start.23 = (s32[3]{0:T(128)}, s32[3]{0:T(128)S(1)}, u32[]{:S(2)}) copy-start(s32[3]{0:T(128)S(1)} %get-tuple-element.37) | copy-start | bytes 40
  27.5 4.8 %copy-start.2 = (bf16[3,768,128]{1,2,0:T(8,128)(2,1)}, bf16[3,768,128]{1,2,0:T(8,128)(2,1)S(1)}, u32[]{:S(2)}) copy-start(bf16[3,768,128]{1,2,0:T(8,128)(2,1)S(1)} %maximum_select_fusion) | copy-start | bytes 1769476
  29.3 2.9 %copy-start.9 = (s32[3,768]{1,0:T(4,128)S(1)}, s32[3,768]{1,0:T(4,128)}, u32[]{:S(2)}) copy-start(s32[3,768]{1,0:T(4,128)} %get-tuple-element.11) | copy-start | bytes 27652
  29.3 2.9 %copy-start.16 = (s32[3,384]{1,0:T(4,128)S(1)}, s32[3,384]{1,0:T(4,128)}, u32[]{:S(2)}) copy-start(s32[3,384]{1,0:T(4,128)} %convert_reduce_fusion.5) | copy-start | bytes 13828
  30.6 9.0 %collective-permute-start.1 = (bf16[3,384,128]{1,2,0:T(8,128)(2,1)S(1)}, bf16[3,384,128]{1,2,0:T(8,128)(2,1)S(1)}, u32[]{:S(2)}, u32[]{:S(2)}) collective-permute-start(bf16[3,384,128]{1,2,0:T(8,128)(2,1)S(1)} %bitcast_select_fusion.1), channel_id=1, source_target_pairs={{0,8},{4,12},{8,0},{12,4},{16,24},{20,28},{24,16},{28,20},{1,9},{5... | collective-permute-start | bytes 884744 | tf_op jit(solution)/shard_map/ppermute | solution.py:10
  42.7 15.7 %collective-permute-start.2 = (bf16[3,384,128]{1,2,0:T(8,128)(2,1)}, bf16[3,384,128]{1,2,0:T(8,128)(2,1)}, u32[]{:S(2)}, u32[]{:S(2)}) collective-permute-start(bf16[3,384,128]{1,2,0:T(8,128)(2,1)} %bitcast_select_fusion), channel_id=1, source_target_pairs={{0,16},{4,20},{8,24},{12,28},{16,0},{20,4},{24,8},{28,12},{1,17},{... | collective-permute-start | bytes 884744 | tf_op jit(solution)/shard_map/ppermute | solution.py:10
  54.8 5.0 %copy-start.7 = (bf16[3,96,1,64]{1,3,2,0:T(8,128)(2,1)S(1)}, bf16[3,96,1,64]{1,3,2,0:T(8,128)(2,1)}, u32[]{:S(2)}) copy-start(bf16[3,96,1,64]{1,3,2,0:T(8,128)(2,1)} %copy.76) | copy-start | bytes 110596
  54.8 5.0 %copy-start.8 = (bf16[3,96,1,64]{1,3,2,0:T(8,128)(2,1)S(1)}, bf16[3,96,1,64]{1,3,2,0:T(8,128)(2,1)}, u32[]{:S(2)}) copy-start(bf16[3,96,1,64]{1,3,2,0:T(8,128)(2,1)} %copy.77) | copy-start | bytes 110596
  54.8 5.0 %copy-start.18 = (s32[3,96]{1,0:T(4,128)S(1)}, s32[3,96]{1,0:T(4,128)}, u32[]{:S(2)}) copy-start(s32[3,96]{1,0:T(4,128)} %convert_reduce_fusion.7) | copy-start | bytes 3460
  54.8 5.0 %copy-start.26 = (pred[3]{0:T(512)(128)(4,1)S(1)}, pred[3]{0:T(512)(128)(4,1)}, u32[]{:S(2)}) copy-start(pred[3]{0:T(512)(128)(4,1)} %copy-done.25) | copy-start | bytes 13
  62.2 3.2 %copy-start.6 = (bf16[192,768]{1,0:T(8,128)(2,1)S(1)}, bf16[192,768]{1,0:T(8,128)(2,1)}, u32[]{:S(2)}) copy-start(bf16[192,768]{1,0:T(8,128)(2,1)} %param.12) | copy-start | bytes 884740
  65.3 23.3 %copy-start.5 = (bf16[384,192]{0,1:T(8,128)(2,1)S(1)}, bf16[384,192]{0,1:T(8,128)(2,1)}, u32[]{:S(2)}) copy-start(bf16[384,192]{0,1:T(8,128)(2,1)} %param.9) | copy-start | bytes 442372
  66.6 30.4 %copy-start.28 = (bf16[768,768]{1,0:T(8,128)(2,1)S(1)}, bf16[768,768]{1,0:T(8,128)(2,1)}, u32[]{:S(2)}) copy-start(bf16[768,768]{1,0:T(8,128)(2,1)} %param.14) | copy-start | bytes 3538948
  66.6 30.4 %copy-start.31 = (f32[768]{0:T(1024)S(1)}, f32[768]{0:T(1024)}, u32[]{:S(2)}) copy-start(f32[768]{0:T(1024)} %param.13) | copy-start | bytes 9220
  66.6 55.5 %reduce-scatter.5.cloned.1.call-start = ((), (), s32[]{:S(2)}) async-start(), calls=%async_computation.3 | async-start | bytes 737280 | tf_op jit(solution)/shard_map/reduce_scatter | solution.py:150
  (15 other events, 17.0 us)
Sparse Core Ops, SparseCore 0:
  66.8 21.8 reduce-scatter.2
  99.6 22.4 reduce-scatter.4
where the time goes:
time: 131 us
  waiting for transfers between devices  51.9 us (40%)
  local copies, waits for them, and re-layouts  16.5 us (13%)
  blocking collectives  16.5 us (13%)
  between operations  14 us (11%)
  other arithmetic  13.5 us (10%)
  matrix products  12.3 us (9%)
  starting transfers between devices  5.83 us (4%)
    reduce_scatter x1, waiting for transfers between devices, local(): lax.psum_scatter(jnp.dot(hidden, second_feed_weight, preferred_element_ty...  22.6 us
    reduce_scatter x1, waiting for transfers between devices, local(): lax.psum_scatter(partial_out.astype(jnp.bfloat16), 'head', scatter_dimens...  22 us
    all_gather x1, blocking collectives, local(): lax.all_gather(tiles, 'head', axis=1, tiled=True).astype(jnp.float32)  9.35 us
    ppermute x3, waiting for transfers between devices, from_partner(): lax.ppermute(array, axis, [(i, i ^ 1 << stride) for i in range(lax.axis_s...  7.3 us
    all_gather x1, blocking collectives, local(): resid_full = lax.all_gather(resid_own, 'head', axis=1, tiled=True)  7.13 us
    ppermute x3, starting transfers between devices, from_partner(): lax.ppermute(array, axis, [(i, i ^ 1 << stride) for i in range(lax.axis_s...  5.79 us
    dot_general x3, matrix products, sparse_dilated_attention(): jnp.einsum('hqk,hkd->hqd', expo.astype(jnp.bfloat16), keyed[:, :, HDIM:],...  4.05 us
    dot_general x3, matrix products, sparse_dilated_attention(): jnp.einsum('hqd,hkd->hqk', queries, keyed[:, :, :HDIM], preferred_element...  3.83 us
  transfers between devices with their start and end apart: 5, of which 4 were waited for; matrix products, arithmetic and copies ran while one was open for 16% of the time, Pallas kernels for 0%

commit v1 on v0

v1 whole, which is shorter than its diff:
```python
import functools

import jax
import jax.numpy as jnp
from jax import lax
from jax.experimental import pallas as pl
from jax.experimental.pallas import tpu as pltpu
from jax.sharding import PartitionSpec as P

HDIM = 64
WIDE = 2 * HDIM
CHUNK = 128
MASKED = -1e30
F32 = jnp.float32
BF16 = jnp.bfloat16


def dot(left, right):
    return jnp.dot(left, right, preferred_element_type=F32)


def padded_rows(rows, level):
    return -(-(rows >> level) // 16) * 16


def key_layout(rows, tile_count):
    pieces, start = {}, rows
    for m in range(1, tile_count):
        level = m.bit_length() - 1
        count = padded_rows(rows, level)
        pieces[m] = (level, start, count)
        start += count
    return pieces, start


def layer_norm_blocks(blocks, gains, width):
    total = sum(jnp.sum(b, axis=-1, keepdims=True) for b in blocks)
    squares = sum(jnp.sum(b * b, axis=-1, keepdims=True) for b in blocks)
    center = total / width
    scale = lax.rsqrt(squares / width - center * center + 1e-05)
    return [((b - center) * scale * g).astype(BF16) for b, g in zip(blocks, gains)]


def kernel(
    tile_count,
    group_count,
    slide_count,
    tiles_ref,
    gain1_ref,
    qkv_hbm,
    wo_hbm,
    gain2_ref,
    w1_hbm,
    w2_hbm,
    counts_ref,
    offsets_ref,
    out_ref,
    wqkv,
    wo,
    w1,
    w2,
    wo_split,
    w2_split,
    xfull,
    rfull,
    qaug,
    kvbuf,
    select_buf,
    top_buf,
    acc_buf,
    attn_buf,
    keep_buf,
    side_send,
    side_recv,
    far_send,
    far_recv,
    load_sem,
    send_sem,
    recv_sem,
):
    rows, share = tiles_ref.shape
    heads = offsets_ref.shape[0]
    levels = tile_count.bit_length() - 1
    chunks = rows // CHUNK
    width = share * group_count
    pieces, key_rows = key_layout(rows, tile_count)
    t = lax.axis_index("tile")
    h = lax.axis_index("head")
    sib, far, diag = h ^ 1, h ^ 2, h ^ 3

    loads = [
        pltpu.make_async_copy(src, dst, load_sem.at[i])
        for i, (src, dst) in enumerate(((qkv_hbm, wqkv), (wo_hbm, wo), (w1_hbm, w1), (w2_hbm, w2)))
    ]
    for load in loads:
        load.start()

    barrier = pltpu.get_barrier_semaphore()
    for peer in (sib, far):
        pl.semaphore_signal(
            barrier, inc=1, device_id=(t, peer), device_id_type=pl.DeviceIdType.MESH
        )
    for m in range(1, tile_count):
        pl.semaphore_signal(
            barrier, inc=1, device_id=(t ^ m, h), device_id_type=pl.DeviceIdType.MESH
        )
    pl.semaphore_wait(barrier, tile_count + 1)

    used = [0]
    sent = []

    def send(src, dst, tile, head):
        index = used[0]
        used[0] += 1
        copy = pltpu.make_async_remote_copy(
            src_ref=src,
            dst_ref=dst,
            send_sem=send_sem.at[index],
            recv_sem=recv_sem.at[index],
            device_id=(tile, head),
            device_id_type=pl.DeviceIdType.MESH,
        )
        copy.start()
        sent.append(copy)
        return copy

    def span(c):
        return pl.ds(c * CHUNK, CHUNK)

    own_far, own_side = [], []
    for c in range(chunks):
        own_far.append(send(tiles_ref.at[span(c)], xfull.at[h, span(c)], t, far))
        own_side.append(send(tiles_ref.at[span(c)], xfull.at[h, span(c)], t, sib))

    lane_row = lax.broadcasted_iota(jnp.int32, (1, WIDE), 1)
    low = jnp.full((1, WIDE), -1, jnp.int32)
    high = jnp.full((1, WIDE), 1 << 30, jnp.int32)
    total = jnp.int32(0)
    for j in range(slide_count - 1):
        total = total + counts_ref[j]
        high = jnp.where(lane_row == HDIM + j, total, high)
        low = jnp.where(lane_row == HDIM + j + 1, total, low)
    is_slide = (lane_row >= HDIM) & (lane_row < HDIM + slide_count)

    def row_iota(count):
        return lax.broadcasted_iota(jnp.int32, (count, WIDE), 0)

    def lane_iota(count):
        return lax.broadcasted_iota(jnp.int32, (count, WIDE), 1)

    offs = [offsets_ref[i] for i in range(heads)]

    def query_features(i):
        posn = t * rows + row_iota(rows)
        lane = lane_iota(rows)
        inside = (posn >= low) & (posn < high) & is_slide
        feats = jnp.where(inside, F32(1), F32(0))
        for level in range(1, levels):
            step = 1 << level
            other = (posn & (step - 1)) != (offs[i] & (step - 1))
            feats = jnp.where((lane == HDIM + slide_count + level - 1) & other, F32(1), feats)
        return feats

    for i in range(heads):
        qaug[i] = query_features(i).astype(BF16)

    for load in loads[:2]:
        load.wait()
    for b in range(group_count):
        wo_split[b] = wo[:, b * share : (b + 1) * share]
    for load in loads[2:]:
        load.wait()
    for b in range(group_count):
        w2_split[b] = w2[:, b * share : (b + 1) * share]

    def project(c, passed):
        own_side[c].wait_recv()
        passed.wait_recv()
        blocks = [
            jnp.where(
                h == b, tiles_ref[span(c)].astype(F32), xfull[b, span(c)].astype(F32)
            )
            for b in range(group_count)
        ]
        normed = layer_norm_blocks(blocks, [gain1_ref[b : b + 1] for b in range(group_count)], width)
        parts = []
        for kind in range(3):
            acc = None
            for b in range(group_count):
                term = dot(normed[b], wqkv[kind, b * share : (b + 1) * share, :])
                acc = term if acc is None else acc + term
            parts.append(acc)
        query, key, value = parts
        query = query.astype(BF16).astype(F32) * F32(HDIM ** (-0.5))
        for i in range(heads):
            own = slice(i * HDIM, (i + 1) * HDIM)
            qaug[i, span(c), 0:HDIM] = query[:, own].astype(BF16)
            kvbuf[i, span(c), 0:HDIM] = key[:, own].astype(BF16)
            kvbuf[i, span(c), HDIM:WIDE] = value[:, own].astype(BF16)

    passed = []
    for c in range(chunks):
        own_far[c].wait_recv()
        passed.append(send(xfull.at[far, span(c)], xfull.at[far, span(c)], t, sib))
        if c > 0:
            project(c - 1, passed[c - 1])
    project(chunks - 1, passed[chunks - 1])

    key_copy = {}

    def send_piece(m):
        level, start, count = pieces[m]
        if level == 0:
            src = kvbuf.at[:, pl.ds(0, count)]
        else:
            src = select_buf.at[:, pl.ds(select_start[level], count)]
        key_copy[m] = send(src, kvbuf.at[:, pl.ds(start, count)], t ^ m, h)

    select_start, at = {}, 0
    for level in range(1, levels):
        select_start[level] = at
        at += padded_rows(rows, level)
    send_piece(1)
    for level in range(levels - 1, 0, -1):
        count = padded_rows(rows, level)
        step = 1 << level
        want = lax.broadcasted_iota(jnp.int32, (count, rows), 0) * step
        have = lax.broadcasted_iota(jnp.int32, (count, rows), 1)
        for i in range(heads):
            pick = jnp.where(have == want + (offs[i] & (step - 1)), F32(1), F32(0)).astype(BF16)
            select_buf[i, pl.ds(select_start[level], count), :] = dot(
                pick, kvbuf[i, pl.ds(0, rows), :]
            ).astype(BF16)
        for m in range(1 << level, 2 << level):
            send_piece(m)

    def attend(i, members, level, first):
        off = offs[i]
        step = 1 << level
        augs, posns, keys = [], [], []
        for m in members:
            if m == 0:
                start, count = 0, rows
            else:
                _, start, count = pieces[m]
            local = row_iota(count) * step + (off & (step - 1))
            posn = (t ^ m) * rows + local
            both = kvbuf[i, pl.ds(start, count), :].astype(F32)
            inside = (posn >= low) & (posn < high) & (local < rows)
            feats = jnp.where(is_slide & jnp.logical_not(inside), F32(MASKED), F32(0))
            if level > 0:
                feats = jnp.where(
                    lane_iota(count) == HDIM + slide_count + level - 1, F32(MASKED), feats
                )
            augs.append(jnp.where(lane_iota(count) < HDIM, both, feats).astype(BF16))
            keys.append(both)
            posns.append(posn)
        aug = augs[0] if len(augs) == 1 else jnp.concatenate(augs, axis=0)
        both = keys[0] if len(keys) == 1 else jnp.concatenate(keys, axis=0)
        posn = posns[0] if len(posns) == 1 else jnp.concatenate(posns, axis=0)
        scores = lax.dot_general(
            qaug[i], aug, (((1,), (1,)), ((), ())), preferred_element_type=F32
        )
        top = jnp.max(scores, axis=1, keepdims=True)
        if not first:
            before = top_buf[i][:, 0:1]
            top = jnp.maximum(top, before)
        expo = jnp.exp(scores - top).astype(BF16)
        summed = jnp.where(lane_iota(both.shape[0]) < HDIM, F32(1), both)
        acc = None
        query_posn = t * rows + row_iota(rows)
        for l in range(level, levels):
            mod = (1 << l) - 1
            weights = summed
            if l > level:
                weights = jnp.where((posn & mod) == (off & mod), summed, F32(0))
            term = dot(expo, weights.astype(BF16))
            if l > 0:
                term = jnp.where((query_posn & mod) == (off & mod), term, F32(0))
            acc = term if acc is None else acc + term
        if not first:
            acc = acc + acc_buf[i] * jnp.exp(before - top)
        acc_buf[i] = acc
        top_buf[i] = jnp.broadcast_to(top, (rows, WIDE))

    for i in range(heads):
        attend(i, [0], 0, True)
    for level in range(levels):
        members = list(range(1 << level, 2 << level))
        for m in members:
            key_copy[m].wait_recv()
        for i in range(heads):
            attend(i, members, level, False)
    for i in range(heads):
        acc = acc_buf[i]
        attn_buf[i] = (acc[:, HDIM:WIDE] / acc[:, 0:1]).astype(BF16)

    side1, far1, side2, far2 = {}, {}, {}, {}
    res_far, res_side, res_pass = {}, {}, {}

    def spread_terms(which, c, block):
        for j, to in enumerate((sib, diag)):
            side_send[which, c, j] = block(to).astype(BF16)
        copy = send(side_send.at[which, c], side_recv.at[which, c], t, sib)
        for j, to in enumerate((far, h)):
            keep_buf[which, c, j] = block(to)
        return copy

    def cross(which, c, side):
        side.wait_recv()
        far_send[which, c] = (
            keep_buf[which, c, 0].astype(BF16).astype(F32) + side_recv[which, c, 1].astype(F32)
        ).astype(BF16)
        return send(far_send.at[which, c], far_recv.at[which, c], t, far)

    def gathered(which, c):
        return (
            keep_buf[which, c, 1].astype(BF16).astype(F32)
            + side_recv[which, c, 0].astype(F32)
            + far_recv[which, c].astype(F32)
        )

    def stage_out(c):
        def block(to):
            acc = None
            for i in range(heads):
                term = dot(attn_buf[i, span(c), :], wo_split[to, i * HDIM : (i + 1) * HDIM, :])
                acc = term if acc is None else acc + term
            return acc

        side1[c] = spread_terms(0, c, block)

    def stage_cross1(c):
        far1[c] = cross(0, c, side1[c])

    def stage_resid(c):
        far1[c].wait_recv()
        rfull[h, span(c)] = (tiles_ref[span(c)].astype(F32) + gathered(0, c)).astype(BF16)
        res_far[c] = send(rfull.at[h, span(c)], rfull.at[h, span(c)], t, far)
        res_side[c] = send(rfull.at[h, span(c)], rfull.at[h, span(c)], t, sib)

    def stage_pass(c):
        res_far[c].wait_recv()
        res_pass[c] = send(rfull.at[far, span(c)], rfull.at[far, span(c)], t, sib)

    def stage_feed(c):
        res_side[c].wait_recv()
        res_pass[c].wait_recv()
        blocks = [rfull[b, span(c)].astype(F32) for b in range(group_count)]
        normed = layer_norm_blocks(blocks, [gain2_ref[b : b + 1] for b in range(group_count)], width)
        acc = None
        for b in range(group_count):
            term = dot(normed[b], w1[b * share : (b + 1) * share, :])
            acc = term if acc is None else acc + term
        hidden = jax.nn.gelu(acc).astype(BF16)
        side2[c] = spread_terms(1, c, lambda to: dot(hidden, w2_split[to]))

    def stage_cross2(c):
        far2[c] = cross(1, c, side2[c])

    def stage_last(c):
        far2[c].wait_recv()
        out_ref[span(c)] = (rfull[h, span(c)].astype(F32) + gathered(1, c)).astype(BF16)

    stages = [
        stage_out,
        stage_cross1,
        stage_resid,
        stage_pass,
        stage_feed,
        stage_cross2,
        stage_last,
    ]
    for step in range(chunks + len(stages) - 1):
        for place in range(len(stages) - 1, -1, -1):
            c = step - place
            if 0 <= c < chunks:
                stages[place](c)
    for copy in sent:
        copy.wait_send()


def local(
    tile_count,
    group_count,
    tiles,
    first_norm_gain,
    query_key_value_weight,
    attention_out_weight,
    second_norm_gain,
    first_feed_weight,
    second_feed_weight,
    slide_tile_counts,
    dilation_head_offsets,
):
    rows, share = tiles.shape
    heads = dilation_head_offsets.shape[0]
    levels = tile_count.bit_length() - 1
    chunks = rows // CHUNK
    _, key_rows = key_layout(rows, tile_count)
    select_rows = max(16, sum(padded_rows(rows, level) for level in range(1, levels)))
    copies = 10 * chunks + tile_count - 1
    vmem = pl.BlockSpec(memory_space=pltpu.VMEM)
    smem = pl.BlockSpec(memory_space=pltpu.SMEM)
    anywhere = pl.BlockSpec(memory_space=pl.ANY)
    hidden = first_feed_weight.shape[1]
    width = share * group_count
    return pl.pallas_call(
        functools.partial(kernel, tile_count, group_count, slide_tile_counts.shape[0]),
        out_shape=jax.ShapeDtypeStruct((rows, share), BF16),
        in_specs=[vmem, vmem, anywhere, anywhere, vmem, anywhere, anywhere, smem, smem],
        out_specs=vmem,
        scratch_shapes=[
            pltpu.VMEM((3, width, share), BF16),
            pltpu.VMEM((share, width), BF16),
            pltpu.VMEM((width, hidden), BF16),
            pltpu.VMEM((hidden, width), BF16),
            pltpu.VMEM((group_count, share, share), BF16),
            pltpu.VMEM((group_count, hidden, share), BF16),
            pltpu.VMEM((group_count, rows, share), BF16),
            pltpu.VMEM((group_count, rows, share), BF16),
            pltpu.VMEM((heads, rows, WIDE), BF16),
            pltpu.VMEM((heads, key_rows, WIDE), BF16),
            pltpu.VMEM((heads, select_rows, WIDE), BF16),
            pltpu.VMEM((heads, rows, WIDE), F32),
            pltpu.VMEM((heads, rows, WIDE), F32),
            pltpu.VMEM((heads, rows, HDIM), BF16),
            pltpu.VMEM((2, chunks, 2, CHUNK, share), F32),
            pltpu.VMEM((2, chunks, 2, CHUNK, share), BF16),
            pltpu.VMEM((2, chunks, 2, CHUNK, share), BF16),
            pltpu.VMEM((2, chunks, CHUNK, share), BF16),
            pltpu.VMEM((2, chunks, CHUNK, share), BF16),
            pltpu.SemaphoreType.DMA((4,)),
            pltpu.SemaphoreType.DMA((copies,)),
            pltpu.SemaphoreType.DMA((copies,)),
        ],
        compiler_params=pltpu.CompilerParams(
            collective_id=0, has_side_effects=True, vmem_limit_bytes=48 << 20
        ),
    )(
        tiles,
        first_norm_gain.reshape(group_count, share),
        jnp.transpose(query_key_value_weight, (1, 0, 2)),
        attention_out_weight,
        second_norm_gain.reshape(group_count, share),
        first_feed_weight,
        second_feed_weight,
        slide_tile_counts,
        dilation_head_offsets,
    )


def solution(mesh):
    return jax.shard_map(
        functools.partial(local, mesh.shape["tile"], mesh.shape["head"]),
        mesh=mesh,
        in_specs=(
            P("tile", "head"),
            P(),
            P(None, None, "head"),
            P("head", None),
            P(),
            P(None, "head"),
            P("head", None),
            P(),
            P("head"),
        ),
        out_specs=P("tile", "head"),
        check_vma=False,
    )
```

time: 131 us -> 69.4 us (0.53)
  Pallas kernels: 0 us -> 59.9 us
  waiting for transfers between devices: 51.9 us -> 0 us
  blocking collectives: 16.5 us -> 0 us
  between operations: 14 us -> 0.08 us
  other arithmetic: 13.5 us -> 0 us
  matrix products: 12.3 us -> 0 us
  local copies, waits for them, and re-layouts: 16.5 us -> 9.17 us
  starting transfers between devices: 5.83 us -> 0 us
    pallas_call x0 -> x1, Pallas kernels: none -> 59.9 us  [local(): pl.pallas_call(functools.partial(kernel, tile_count, group_count, slide_t...]
    reduce_scatter x2 -> x0, waiting for transfers between devices: 44.6 us -> none  [the longest x1 22.6 us: local(): lax.psum_scatter(jnp.dot(hidden, second_feed_weight, preferred_element_ty...]
    all_gather x2 -> x0, blocking collectives: 16.5 us -> none  [the longest x1 9.35 us: local(): lax.all_gather(tiles, 'head', axis=1, tiled=True).astype(jnp.float32)]
    dot_general x8 -> x0, matrix products: 11.6 us -> none  [the longest x3 4.05 us: sparse_dilated_attention(): jnp.einsum('hqk,hkd->hqd', expo.astype(jnp.bfloat16), keyed[:, :, HDIM:],...]
    ppermute x3 -> x0, waiting for transfers between devices: 7.3 us -> none  [from_partner(): lax.ppermute(array, axis, [(i, i ^ 1 << stride) for i in range(lax.axis_s...]
    reduce_sum x9 -> x0, other arithmetic: 6.27 us -> none  [the longest x3 3.14 us: sparse_dilated_attention(): sums = jnp.sum(expo, axis=2)]
    ppermute x3 -> x0, starting transfers between devices: 5.79 us -> none  [from_partner(): lax.ppermute(array, axis, [(i, i ^ 1 << stride) for i in range(lax.axis_s...]
    slice x10 -> x0, local copies, waits for them, and re-layouts: 5.54 us -> none  [the longest x5 3.36 us: take_half(): shaped[:, :, 0]]
  transfers between devices with their start and end apart: 5 -> 0, of which waited for: 4 -> 0; matrix products, arithmetic and copies ran while one was open for 16% -> 0% of each run, Pallas kernels for 0% -> 0%
where the time goes in v1:
time: 69.4 us; the launch traced here: 69.1 us
  Pallas kernels  59.9 us (86%)
  local copies, waits for them, and re-layouts  9.17 us (13%)
    pallas_call x1, Pallas kernels, local(): pl.pallas_call(functools.partial(kernel, tile_count, group_count, slide_t...  59.9 us
    unnamed x16, local copies, waits for them, and re-layouts  5.94 us
    pallas_call x1, local copies, waits for them, and re-layouts, local(): pl.pallas_call(functools.partial(kernel, tile_count, group_count, slide_t...  1.71 us

profile of v1, /device:TPU:0, one launch (start us, length us, event | category | flops | bytes accessed | tf_op | source)
XLA Modules:
  0.0 69.1 jit_solution(9159969908578851504)
XLA Ops:
  0.0 0.8 %reshape.6.gain1_ref = f32[4,192]{1,0:T(4,128)S(1)} reshape(f32[768]{0:T(1024)} %param.10) | data formatting | bytes 6144 | tf_op jit(solution)/shard_map/reshape | solution.py:442
  0.8 0.8 %reshape.7.gain2_ref = f32[4,192]{1,0:T(4,128)S(1)} reshape(f32[768]{0:T(1024)} %param.13) | data formatting | bytes 6144 | tf_op jit(solution)/shard_map/reshape | solution.py:445
  1.5 0.0 copy-start
  1.5 0.0 copy-start.1
  1.5 0.0 copy-start.5
  1.5 0.0 copy-start.6
  1.5 1.9 %copy.11.tiles_ref = bf16[384,192]{1,0:T(8,128)(2,1)} copy(bf16[384,192]{0,1:T(8,128)(2,1)} %param.9) | data formatting | bytes 294912 | tf_op args[0]
  3.4 1.5 %copy.10 = bf16[768,3,192]{2,0,1:T(8,128)(2,1)S(1)} copy(bf16[768,3,192]{0,2,1:T(8,128)(2,1)} %param.11) | data formatting | bytes 1769472 | tf_op args[2]
  4.9 0.0 copy-done
  4.9 0.0 copy-done.1
  5.0 0.0 copy-done.5
  5.0 0.0 copy-done.6
  5.0 0.0 copy-start.3
  5.0 0.9 %copy-done.3 = bf16[384,192]{1,0:T(8,128)(2,1)S(1)} copy-done((bf16[384,192]{1,0:T(8,128)(2,1)S(1)}, bf16[384,192]{1,0:T(8,128)(2,1)}, u32[]{:S(2)}) %copy-start.3) | copy-done | bytes 147480
  5.9 0.0 copy-start.4
  5.9 1.0 %copy-done.4 = bf16[192,768]{1,0:T(8,128)(2,1)S(1)} copy-done((bf16[192,768]{1,0:T(8,128)(2,1)S(1)}, bf16[192,768]{1,0:T(8,128)(2,1)}, u32[]{:S(2)}) %copy-start.4) | copy-done | bytes 294936
  6.9 59.9 %shard_map.91 = bf16[384,192]{1,0:T(8,128)(2,1)S(1)} custom-call(bf16[384,192]{1,0:T(8,128)(2,1)S(1)} %copy-done.3, f32[4,192]{1,0:T(4,128)S(1)} %reshape.6.gain1_ref, bf16[3,768,192]{2,1,0:T(8,128)(2,1)S(1)} %bitcast.1, bf16[192,768]{1,0:T(8,128)(2,1)S(1)} %copy-done.4, f32[4,192]{1,0:T(4,128)S(1)} %reshape.7.gain2_ref, bf16[768,768]{1,0:T(8,128)(2,1)S(1)} %copy-done, ...), custom_call_target="tpu_custom_call" | custom-call | tf_op jit(solution)/shard_map/pallas_call | solution.py:408
  66.8 0.0 copy-start.2
  66.8 0.7 copy-done.2
  67.4 1.7 %copy.12 = bf16[384,192]{0,1:T(8,128)(2,1)} copy(bf16[384,192]{1,0:T(8,128)(2,1)} %copy-done.2) | data formatting | bytes 294912 | tf_op jit(solution)/shard_map/pallas_call | solution.py:408
Async XLA Ops:
  1.5 3.4 %copy-start = (bf16[768,768]{1,0:T(8,128)(2,1)S(1)}, bf16[768,768]{1,0:T(8,128)(2,1)}, u32[]{:S(2)}) copy-start(bf16[768,768]{1,0:T(8,128)(2,1)} %w1_hbm.1) | copy-start | bytes 3538948
  1.5 3.4 %copy-start.1 = (bf16[768,768]{1,0:T(8,128)(2,1)S(1)}, bf16[768,768]{1,0:T(8,128)(2,1)}, u32[]{:S(2)}) copy-start(bf16[768,768]{1,0:T(8,128)(2,1)} %w2_hbm.1) | copy-start | bytes 3538948
  1.5 3.4 %copy-start.5 = (s32[6]{0:T(128)S(1)}, s32[6]{0:T(128)}, u32[]{:S(2)}) copy-start(s32[6]{0:T(128)} %counts_ref.1) | copy-start | bytes 76
  1.5 3.4 %copy-start.6 = (s32[3]{0:T(128)S(1)}, s32[3]{0:T(128)}, u32[]{:S(2)}) copy-start(s32[3]{0:T(128)} %offsets_ref.1) | copy-start | bytes 40
  5.0 0.9 %copy-start.3 = (bf16[384,192]{1,0:T(8,128)(2,1)S(1)}, bf16[384,192]{1,0:T(8,128)(2,1)}, u32[]{:S(2)}) copy-start(bf16[384,192]{1,0:T(8,128)(2,1)} %copy.11.tiles_ref) | copy-start | bytes 442372
  5.9 1.0 %copy-start.4 = (bf16[192,768]{1,0:T(8,128)(2,1)S(1)}, bf16[192,768]{1,0:T(8,128)(2,1)}, u32[]{:S(2)}) copy-start(bf16[192,768]{1,0:T(8,128)(2,1)} %wo_hbm.1) | copy-start | bytes 884740
  66.8 0.7 copy-start.2

commit v2 on v1

--- a/solution.py
+++ b/solution.py
@@ -33,34 +33,42 @@
     return pieces, start
 
 
-def layer_norm_blocks(blocks, gains, width):
-    total = sum(jnp.sum(b, axis=-1, keepdims=True) for b in blocks)
-    squares = sum(jnp.sum(b * b, axis=-1, keepdims=True) for b in blocks)
-    center = total / width
-    scale = lax.rsqrt(squares / width - center * center + 1e-05)
-    return [((b - center) * scale * g).astype(BF16) for b, g in zip(blocks, gains)]
+def layer_norm_columns(values, gain):
+    width = values.shape[0]
+    center = jnp.sum(values, axis=0, keepdims=True) / width
+    square = jnp.sum(values * values, axis=0, keepdims=True) / width
+    scale = lax.rsqrt(square - center * center + 1e-05)
+    return ((values - center) * scale * gain).astype(BF16)
 
 
 def kernel(
     tile_count,
     group_count,
     slide_count,
-    tiles_ref,
-    gain1_ref,
+    tiles_hbm,
+    gain1_hbm,
     qkv_hbm,
     wo_hbm,
-    gain2_ref,
+    gain2_hbm,
     w1_hbm,
     w2_hbm,
+    counts_hbm,
+    offsets_hbm,
+    out_ref,
+    tiles_ref,
+    gain1_row,
+    gain2_row,
+    gain1,
+    gain2,
     counts_ref,
     offsets_ref,
-    out_ref,
     wqkv,
     wo,
     w1,
     w2,
-    wo_split,
-    w2_split,
+    wo_turned,
+    w1_turned,
+    w2_turned,
     xfull,
     rfull,
     qaug,
@@ -78,7 +86,7 @@
     send_sem,
     recv_sem,
 ):
-    rows, share = tiles_ref.shape
+    share, rows = tiles_ref.shape
     heads = offsets_ref.shape[0]
     levels = tile_count.bit_length() - 1
     chunks = rows // CHUNK
@@ -90,7 +98,19 @@
 
     loads = [
         pltpu.make_async_copy(src, dst, load_sem.at[i])
-        for i, (src, dst) in enumerate(((qkv_hbm, wqkv), (wo_hbm, wo), (w1_hbm, w1), (w2_hbm, w2)))
+        for i, (src, dst) in enumerate(
+            (
+                (tiles_hbm, tiles_ref),
+                (counts_hbm, counts_ref),
+                (offsets_hbm, offsets_ref),
+                (gain1_hbm, gain1_row),
+                (gain2_hbm, gain2_row),
+                (wo_hbm, wo),
+                (w1_hbm, w1),
+                (w2_hbm, w2),
+                (qkv_hbm, wqkv),
+            )
+        )
     ]
     for load in loads:
         load.start()
@@ -127,10 +147,14 @@
     def span(c):
         return pl.ds(c * CHUNK, CHUNK)
 
+    loads[0].wait()
     own_far, own_side = [], []
     for c in range(chunks):
-        own_far.append(send(tiles_ref.at[span(c)], xfull.at[h, span(c)], t, far))
-        own_side.append(send(tiles_ref.at[span(c)], xfull.at[h, span(c)], t, sib))
+        own_far.append(send(tiles_ref.at[:, span(c)], xfull.at[c, h], t, far))
+    for c in range(chunks):
+        own_side.append(send(tiles_ref.at[:, span(c)], xfull.at[c, h], t, sib))
+    loads[1].wait()
+    loads[2].wait()
 
     lane_row = lax.broadcasted_iota(jnp.int32, (1, WIDE), 1)
     low = jnp.full((1, WIDE), -1, jnp.int32)
@@ -164,47 +188,44 @@
     for i in range(heads):
         qaug[i] = query_features(i).astype(BF16)
 
-    for load in loads[:2]:
+    for load in loads[3:]:
         load.wait()
+    gain1[...] = jnp.broadcast_to(gain1_row[...][None], (CHUNK, width)).T
+    gain2[...] = jnp.broadcast_to(gain2_row[...][None], (CHUNK, width)).T
+    turned = wo[...].T
     for b in range(group_count):
-        wo_split[b] = wo[:, b * share : (b + 1) * share]
-    for load in loads[2:]:
-        load.wait()
+        wo_turned[b] = turned[b * share : (b + 1) * share]
+    w1_turned[...] = w1[...].T
+    turned = w2[...].T
     for b in range(group_count):
-        w2_split[b] = w2[:, b * share : (b + 1) * share]
+        w2_turned[b] = turned[b * share : (b + 1) * share]
+
+    def columns(blocks):
+        return jnp.concatenate(blocks, axis=0).astype(F32)
 
     def project(c, passed):
         own_side[c].wait_recv()
         passed.wait_recv()
-        blocks = [
-            jnp.where(
-                h == b, tiles_ref[span(c)].astype(F32), xfull[b, span(c)].astype(F32)
-            )
-            for b in range(group_count)
-        ]
-        normed = layer_norm_blocks(blocks, [gain1_ref[b : b + 1] for b in range(group_count)], width)
-        parts = []
-        for kind in range(3):
-            acc = None
-            for b in range(group_count):
-                term = dot(normed[b], wqkv[kind, b * share : (b + 1) * share, :])
-                acc = term if acc is None else acc + term
-            parts.append(acc)
-        query, key, value = parts
+        own = tiles_ref[:, span(c)]
+        blocks = [jnp.where(h == b, own, xfull[c, b]) for b in range(group_count)]
+        normed = layer_norm_columns(columns(blocks), gain1[...])
+        query, key, value = [dot(wqkv[kind], normed) for kind in range(3)]
         query = query.astype(BF16).astype(F32) * F32(HDIM ** (-0.5))
         for i in range(heads):
             own = slice(i * HDIM, (i + 1) * HDIM)
-            qaug[i, span(c), 0:HDIM] = query[:, own].astype(BF16)
-            kvbuf[i, span(c), 0:HDIM] = key[:, own].astype(BF16)
-            kvbuf[i, span(c), HDIM:WIDE] = value[:, own].astype(BF16)
+            features = jnp.concatenate([query[own], query[own]], axis=0).T
+            first = lane_iota(CHUNK) < HDIM
+            qaug[i, span(c), :] = jnp.where(
+                first, features, qaug[i, span(c), :].astype(F32)
+            ).astype(BF16)
+            kvbuf[i, span(c), :] = jnp.concatenate([key[own], value[own]], axis=0).T.astype(BF16)
 
     passed = []
     for c in range(chunks):
         own_far[c].wait_recv()
-        passed.append(send(xfull.at[far, span(c)], xfull.at[far, span(c)], t, sib))
-        if c > 0:
-            project(c - 1, passed[c - 1])
-    project(chunks - 1, passed[chunks - 1])
+        passed.append(send(xfull.at[c, far], xfull.at[c, far], t, sib))
+    for c in range(chunks):
+        project(c, passed[c])
 
     key_copy = {}
 
@@ -292,8 +313,8 @@
         for i in range(heads):
             attend(i, members, level, False)
     for i in range(heads):
-        acc = acc_buf[i]
-        attn_buf[i] = (acc[:, HDIM:WIDE] / acc[:, 0:1]).astype(BF16)
+        acc = acc_buf[i].T
+        attn_buf[i * HDIM : (i + 1) * HDIM] = (acc[HDIM:WIDE] / acc[0:1]).astype(BF16)
 
     side1, far1, side2, far2 = {}, {}, {}, {}
     res_far, res_side, res_pass = {}, {}, {}
@@ -321,46 +342,36 @@
         )
 
     def stage_out(c):
-        def block(to):
-            acc = None
-            for i in range(heads):
-                term = dot(attn_buf[i, span(c), :], wo_split[to, i * HDIM : (i + 1) * HDIM, :])
-                acc = term if acc is None else acc + term
-            return acc
-
-        side1[c] = spread_terms(0, c, block)
+        attn = attn_buf[:, span(c)]
+        side1[c] = spread_terms(0, c, lambda to: dot(wo_turned[to], attn))
 
     def stage_cross1(c):
         far1[c] = cross(0, c, side1[c])
 
     def stage_resid(c):
         far1[c].wait_recv()
-        rfull[h, span(c)] = (tiles_ref[span(c)].astype(F32) + gathered(0, c)).astype(BF16)
-        res_far[c] = send(rfull.at[h, span(c)], rfull.at[h, span(c)], t, far)
-        res_side[c] = send(rfull.at[h, span(c)], rfull.at[h, span(c)], t, sib)
+        rfull[c, h] = (tiles_ref[:, span(c)].astype(F32) + gathered(0, c)).astype(BF16)
+        res_far[c] = send(rfull.at[c, h], rfull.at[c, h], t, far)
+        res_side[c] = send(rfull.at[c, h], rfull.at[c, h], t, sib)
 
     def stage_pass(c):
         res_far[c].wait_recv()
-        res_pass[c] = send(rfull.at[far, span(c)], rfull.at[far, span(c)], t, sib)
+        res_pass[c] = send(rfull.at[c, far], rfull.at[c, far], t, sib)
 
     def stage_feed(c):
         res_side[c].wait_recv()
         res_pass[c].wait_recv()
-        blocks = [rfull[b, span(c)].astype(F32) for b in range(group_count)]
-        normed = layer_norm_blocks(blocks, [gain2_ref[b : b + 1] for b in range(group_count)], width)
-        acc = None
-        for b in range(group_count):
-            term = dot(normed[b], w1[b * share : (b + 1) * share, :])
-            acc = term if acc is None else acc + term
-        hidden = jax.nn.gelu(acc).astype(BF16)
-        side2[c] = spread_terms(1, c, lambda to: dot(hidden, w2_split[to]))
+        blocks = [rfull[c, b] for b in range(group_count)]
+        normed = layer_norm_columns(columns(blocks), gain2[...])
+        hidden = jax.nn.gelu(dot(w1_turned[...], normed)).astype(BF16)
+        side2[c] = spread_terms(1, c, lambda to: dot(w2_turned[to], hidden))
 
     def stage_cross2(c):
         far2[c] = cross(1, c, side2[c])
 
     def stage_last(c):
         far2[c].wait_recv()
-        out_ref[span(c)] = (rfull[h, span(c)].astype(F32) + gathered(1, c)).astype(BF16)
+        out_ref[:, span(c)] = (rfull[c, h].astype(F32) + gathered(1, c)).astype(BF16)
 
     stages = [
         stage_out,
@@ -371,11 +382,9 @@
         stage_cross2,
         stage_last,
     ]
-    for step in range(chunks + len(stages) - 1):
-        for place in range(len(stages) - 1, -1, -1):
-            c = step - place
-            if 0 <= c < chunks:
-                stages[place](c)
+    for stage in stages:
+        for c in range(chunks):
+            stage(c)
     for copy in sent:
         copy.wait_send()
 
@@ -401,53 +410,60 @@
     select_rows = max(16, sum(padded_rows(rows, level) for level in range(1, levels)))
     copies = 10 * chunks + tile_count - 1
     vmem = pl.BlockSpec(memory_space=pltpu.VMEM)
-    smem = pl.BlockSpec(memory_space=pltpu.SMEM)
-    anywhere = pl.BlockSpec(memory_space=pl.ANY)
+    hbm = pl.BlockSpec(memory_space=pltpu.HBM)
     hidden = first_feed_weight.shape[1]
     width = share * group_count
     return pl.pallas_call(
         functools.partial(kernel, tile_count, group_count, slide_tile_counts.shape[0]),
-        out_shape=jax.ShapeDtypeStruct((rows, share), BF16),
-        in_specs=[vmem, vmem, anywhere, anywhere, vmem, anywhere, anywhere, smem, smem],
+        out_shape=jax.ShapeDtypeStruct((share, rows), BF16),
+        in_specs=[hbm] * 9,
         out_specs=vmem,
         scratch_shapes=[
-            pltpu.VMEM((3, width, share), BF16),
+            pltpu.VMEM((share, rows), BF16),
+            pltpu.VMEM((width,), F32),
+            pltpu.VMEM((width,), F32),
+            pltpu.VMEM((width, CHUNK), F32),
+            pltpu.VMEM((width, CHUNK), F32),
+            pltpu.SMEM(slide_tile_counts.shape, jnp.int32),
+            pltpu.SMEM(dilation_head_offsets.shape, jnp.int32),
+            pltpu.VMEM((3, share, width), BF16),
             pltpu.VMEM((share, width), BF16),
             pltpu.VMEM((width, hidden), BF16),
             pltpu.VMEM((hidden, width), BF16),
             pltpu.VMEM((group_count, share, share), BF16),
-            pltpu.VMEM((group_count, hidden, share), BF16),
-            pltpu.VMEM((group_count, rows, share), BF16),
-            pltpu.VMEM((group_count, rows, share), BF16),
+            pltpu.VMEM((hidden, width), BF16),
+            pltpu.VMEM((group_count, share, hidden), BF16),
+            pltpu.VMEM((chunks, group_count, share, CHUNK), BF16),
+            pltpu.VMEM((chunks, group_count, share, CHUNK), BF16),
             pltpu.VMEM((heads, rows, WIDE), BF16),
             pltpu.VMEM((heads, key_rows, WIDE), BF16),
             pltpu.VMEM((heads, select_rows, WIDE), BF16),
             pltpu.VMEM((heads, rows, WIDE), F32),
             pltpu.VMEM((heads, rows, WIDE), F32),
-            pltpu.VMEM((heads, rows, HDIM), BF16),
-            pltpu.VMEM((2, chunks, 2, CHUNK, share), F32),
-            pltpu.VMEM((2, chunks, 2, CHUNK, share), BF16),
-            pltpu.VMEM((2, chunks, 2, CHUNK, share), BF16),
-            pltpu.VMEM((2, chunks, CHUNK, share), BF16),
-            pltpu.VMEM((2, chunks, CHUNK, share), BF16),
-            pltpu.SemaphoreType.DMA((4,)),
+            pltpu.VMEM((share, rows), BF16),
+            pltpu.VMEM((2, chunks, 2, share, CHUNK), F32),
+            pltpu.VMEM((2, chunks, 2, share, CHUNK), BF16),
+            pltpu.VMEM((2, chunks, 2, share, CHUNK), BF16),
+            pltpu.VMEM((2, chunks, share, CHUNK), BF16),
+            pltpu.VMEM((2, chunks, share, CHUNK), BF16),
+            pltpu.SemaphoreType.DMA((9,)),
             pltpu.SemaphoreType.DMA((copies,)),
             pltpu.SemaphoreType.DMA((copies,)),
         ],
         compiler_params=pltpu.CompilerParams(
-            collective_id=0, has_side_effects=True, vmem_limit_bytes=48 << 20
+            collective_id=0, has_side_effects=True, vmem_limit_bytes=64 << 20
         ),
     )(
-        tiles,
-        first_norm_gain.reshape(group_count, share),
-        jnp.transpose(query_key_value_weight, (1, 0, 2)),
+        tiles.T,
+        first_norm_gain,
+        jnp.transpose(query_key_value_weight, (1, 2, 0)),
         attention_out_weight,
-        second_norm_gain.reshape(group_count, share),
+        second_norm_gain,
         first_feed_weight,
         second_feed_weight,
         slide_tile_counts,
         dilation_head_offsets,
-    )
+    ).T
 
 
 def solution(mesh):

time: 69.4 us -> 54.7 us (0.79)
  local copies, waits for them, and re-layouts: 9.17 us -> 1.59 us
  Pallas kernels: 59.9 us -> 52.6 us
    pallas_call x1, Pallas kernels: 59.9 us -> 52.6 us  [local(): pl.pallas_call(functools.partial(kernel, tile_count, group_count, slide_t...]
    unnamed x16 -> x1, local copies, waits for them, and re-layouts: 5.94 us -> 1.59 us
    pallas_call x1 -> x0, local copies, waits for them, and re-layouts: 1.71 us -> none  [local(): pl.pallas_call(functools.partial(kernel, tile_count, group_count, slide_t...]
    reshape x2 -> x0, local copies, waits for them, and re-layouts: 1.53 us -> none  [the longest x1 0.76 us: local(): first_norm_gain.reshape(group_count, share)]
where the time goes in v2:
time: 54.7 us; the launch traced here: 54.2 us
  Pallas kernels  52.6 us (96%)
  local copies, waits for them, and re-layouts  1.59 us (3%)
    pallas_call x1, Pallas kernels, local(): pl.pallas_call(functools.partial(kernel, tile_count, group_count, slide_t...  52.6 us
    unnamed x1, local copies, waits for them, and re-layouts  1.59 us

profile of v2, /device:TPU:0, one launch (start us, length us, event | category | flops | bytes accessed | tf_op | source)
XLA Modules:
  0.0 54.2 jit_solution(14923502207416169290)
XLA Ops:
  0.0 52.6 %shard_map.91 = bf16[192,384]{1,0:T(8,128)(2,1)} custom-call(bf16[192,384]{1,0:T(8,128)(2,1)} %bitcast.5, f32[768]{0:T(1024)} %gain1_hbm.1, bf16[3,192,768]{2,1,0:T(8,128)(2,1)} %bitcast.3, bf16[192,768]{1,0:T(8,128)(2,1)} %wo_hbm.1, f32[768]{0:T(1024)} %gain2_hbm.1, bf16[768,768]{1,0:T(8,128)(2,1)} %w1_hbm.1, bf16[768,768]{1,0:T(8,128)(2,1)} %w2_hbm.1, ...), custom_call_target="tpu_custom_call" | custom-call | tf_op jit(solution)/shard_map/pallas_call | solution.py:416
  52.6 1.6 %copy.11 = bf16[384,192]{0,1:T(8,128)(2,1)} copy(bf16[384,192]{0,1:T(8,128)(2,1)} %bitcast.4) | data formatting | bytes 294912

commit v3 on v2

--- a/solution.py
+++ b/solution.py
@@ -21,6 +21,11 @@
 
 def padded_rows(rows, level):
     return -(-(rows >> level) // 16) * 16
+
+
+def key_parts(rows, tile_count):
+    levels = tile_count.bit_length() - 1
+    return rows // CHUNK if (CHUNK >> (levels - 1)) % 16 == 0 else 1
 
 
 def key_layout(rows, tile_count):
@@ -224,38 +229,43 @@
     for c in range(chunks):
         own_far[c].wait_recv()
         passed.append(send(xfull.at[c, far], xfull.at[c, far], t, sib))
-    for c in range(chunks):
-        project(c, passed[c])
-
+    parts = key_parts(rows, tile_count)
     key_copy = {}
-
-    def send_piece(m):
-        level, start, count = pieces[m]
-        if level == 0:
-            src = kvbuf.at[:, pl.ds(0, count)]
-        else:
-            src = select_buf.at[:, pl.ds(select_start[level], count)]
-        key_copy[m] = send(src, kvbuf.at[:, pl.ds(start, count)], t ^ m, h)
-
     select_start, at = {}, 0
     for level in range(1, levels):
         select_start[level] = at
         at += padded_rows(rows, level)
-    send_piece(1)
-    for level in range(levels - 1, 0, -1):
-        count = padded_rows(rows, level)
-        step = 1 << level
-        want = lax.broadcasted_iota(jnp.int32, (count, rows), 0) * step
-        have = lax.broadcasted_iota(jnp.int32, (count, rows), 1)
-        for i in range(heads):
-            pick = jnp.where(have == want + (offs[i] & (step - 1)), F32(1), F32(0)).astype(BF16)
-            select_buf[i, pl.ds(select_start[level], count), :] = dot(
-                pick, kvbuf[i, pl.ds(0, rows), :]
-            ).astype(BF16)
-        for m in range(1 << level, 2 << level):
-            send_piece(m)
-
-    def attend(i, members, level, first):
+
+    def send_keys(part):
+        span_rows = rows // parts
+        source = pl.ds(part * span_rows, span_rows)
+        for level in [0] + list(range(levels - 1, 0, -1)):
+            count = padded_rows(rows, level) // parts
+            if level == 0:
+                src = kvbuf.at[:, source]
+            else:
+                step = 1 << level
+                place = pl.ds(select_start[level] + part * count, count)
+                want = lax.broadcasted_iota(jnp.int32, (count, span_rows), 0) * step
+                have = lax.broadcasted_iota(jnp.int32, (count, span_rows), 1)
+                for i in range(heads):
+                    pick = jnp.where(have == want + (offs[i] & (step - 1)), F32(1), F32(0))
+                    select_buf[i, place, :] = dot(
+                        pick.astype(BF16), kvbuf[i, source, :]
+                    ).astype(BF16)
+                src = select_buf.at[:, place]
+            for m in range(1 << level, 2 << level):
+                start = pieces[m][1] + part * count
+                key_copy[m, part] = send(src, kvbuf.at[:, pl.ds(start, count)], t ^ m, h)
+
+    for c in range(chunks):
+        project(c, passed[c])
+        if parts == chunks:
+            send_keys(c)
+    if parts != chunks:
+        send_keys(0)
+
+    def prepare(i, members, level):
         off = offs[i]
         step = 1 << level
         augs, posns, keys = [], [], []
@@ -279,42 +289,61 @@
         aug = augs[0] if len(augs) == 1 else jnp.concatenate(augs, axis=0)
         both = keys[0] if len(keys) == 1 else jnp.concatenate(keys, axis=0)
         posn = posns[0] if len(posns) == 1 else jnp.concatenate(posns, axis=0)
+        summed = jnp.where(lane_iota(both.shape[0]) < HDIM, F32(1), both)
+        weights = []
+        for l in range(level, levels):
+            mod = (1 << l) - 1
+            chosen = summed
+            if l > level:
+                chosen = jnp.where((posn & mod) == (off & mod), summed, F32(0))
+            weights.append(chosen.astype(BF16))
+        return aug, weights
+
+    def attend(i, prepared, level, first, begin, count):
+        aug, weights = prepared
+        query = pl.ds(begin, count)
         scores = lax.dot_general(
-            qaug[i], aug, (((1,), (1,)), ((), ())), preferred_element_type=F32
+            qaug[i, query, :], aug, (((1,), (1,)), ((), ())), preferred_element_type=F32
         )
         top = jnp.max(scores, axis=1, keepdims=True)
         if not first:
-            before = top_buf[i][:, 0:1]
+            before = top_buf[i, query, 0:1]
             top = jnp.maximum(top, before)
         expo = jnp.exp(scores - top).astype(BF16)
-        summed = jnp.where(lane_iota(both.shape[0]) < HDIM, F32(1), both)
         acc = None
-        query_posn = t * rows + row_iota(rows)
+        query_posn = t * rows + begin + row_iota(count)
         for l in range(level, levels):
             mod = (1 << l) - 1
-            weights = summed
-            if l > level:
-                weights = jnp.where((posn & mod) == (off & mod), summed, F32(0))
-            term = dot(expo, weights.astype(BF16))
+            term = dot(expo, weights[l - level])
             if l > 0:
-                term = jnp.where((query_posn & mod) == (off & mod), term, F32(0))
+                term = jnp.where((query_posn & mod) == (offs[i] & mod), term, F32(0))
             acc = term if acc is None else acc + term
         if not first:
-            acc = acc + acc_buf[i] * jnp.exp(before - top)
-        acc_buf[i] = acc
-        top_buf[i] = jnp.broadcast_to(top, (rows, WIDE))
-
-    for i in range(heads):
-        attend(i, [0], 0, True)
-    for level in range(levels):
+            acc = acc + acc_buf[i, query, :] * jnp.exp(before - top)
+        acc_buf[i, query, :] = acc
+        top_buf[i, query, :] = jnp.broadcast_to(top, (count, WIDE))
+
+    def arrived(level):
         members = list(range(1 << level, 2 << level))
         for m in members:
-            key_copy[m].wait_recv()
+            for part in range(parts):
+                key_copy[m, part].wait_recv()
+        return members
+
+    for i in range(heads):
+        attend(i, prepare(i, [0], 0), 0, True, 0, rows)
+    for level in range(levels - 1):
+        members = arrived(level)
         for i in range(heads):
-            attend(i, members, level, False)
-    for i in range(heads):
-        acc = acc_buf[i].T
-        attn_buf[i * HDIM : (i + 1) * HDIM] = (acc[HDIM:WIDE] / acc[0:1]).astype(BF16)
+            attend(i, prepare(i, members, level), level, False, 0, rows)
+    members = arrived(levels - 1)
+    last_keys = [prepare(i, members, levels - 1) for i in range(heads)]
+
+    def finish(c):
+        for i in range(heads):
+            attend(i, last_keys[i], levels - 1, False, c * CHUNK, CHUNK)
+            acc = acc_buf[i, span(c), :].T
+            attn_buf[i * HDIM : (i + 1) * HDIM, span(c)] = (acc[HDIM:WIDE] / acc[0:1]).astype(BF16)
 
     side1, far1, side2, far2 = {}, {}, {}, {}
     res_far, res_side, res_pass = {}, {}, {}
@@ -342,6 +371,7 @@
         )
 
     def stage_out(c):
+        finish(c)
         attn = attn_buf[:, span(c)]
         side1[c] = spread_terms(0, c, lambda to: dot(wo_turned[to], attn))
 
@@ -373,18 +403,20 @@
         far2[c].wait_recv()
         out_ref[:, span(c)] = (rfull[c, h].astype(F32) + gathered(1, c)).astype(BF16)
 
-    stages = [
-        stage_out,
-        stage_cross1,
-        stage_resid,
-        stage_pass,
-        stage_feed,
-        stage_cross2,
-        stage_last,
-    ]
-    for stage in stages:
+    def staged(ahead, behind):
+        for c in range(chunks + 1):
+            if c < chunks:
+                ahead(c)
+            if c > 0:
+                behind(c - 1)
+
+    staged(stage_out, stage_cross1)
+    for stage in (stage_resid, stage_pass):
         for c in range(chunks):
             stage(c)
+    staged(stage_feed, stage_cross2)
+    for c in range(chunks):
+        stage_last(c)
     for copy in sent:
         copy.wait_send()
 
@@ -408,7 +440,7 @@
     chunks = rows // CHUNK
     _, key_rows = key_layout(rows, tile_count)
     select_rows = max(16, sum(padded_rows(rows, level) for level in range(1, levels)))
-    copies = 10 * chunks + tile_count - 1
+    copies = 10 * chunks + (tile_count - 1) * key_parts(rows, tile_count)
     vmem = pl.BlockSpec(memory_space=pltpu.VMEM)
     hbm = pl.BlockSpec(memory_space=pltpu.HBM)
     hidden = first_feed_weight.shape[1]

time: 54.7 us -> 54.1 us (0.989)
  no operation moved by 1% of the time
where the time goes in v3:
time: 54.1 us; the launch traced here: 53.9 us
  Pallas kernels  52.3 us (97%)
  local copies, waits for them, and re-layouts  1.59 us (3%)
    pallas_call x1, Pallas kernels, local(): pl.pallas_call(functools.partial(kernel, tile_count, group_count, slide_t...  52.3 us
    unnamed x1, local copies, waits for them, and re-layouts  1.59 us

profile of v3, /device:TPU:0, one launch (start us, length us, event | category | flops | bytes accessed | tf_op | source)
XLA Modules:
  0.0 53.9 jit_solution(15346880264003233840)
XLA Ops:
  0.0 52.3 %shard_map.91 = bf16[192,384]{1,0:T(8,128)(2,1)} custom-call(bf16[192,384]{1,0:T(8,128)(2,1)} %bitcast.5, f32[768]{0:T(1024)} %gain1_hbm.1, bf16[3,192,768]{2,1,0:T(8,128)(2,1)} %bitcast.3, bf16[192,768]{1,0:T(8,128)(2,1)} %wo_hbm.1, f32[768]{0:T(1024)} %gain2_hbm.1, bf16[768,768]{1,0:T(8,128)(2,1)} %w1_hbm.1, bf16[768,768]{1,0:T(8,128)(2,1)} %w2_hbm.1, ...), custom_call_target="tpu_custom_call" | custom-call | tf_op jit(solution)/shard_map/pallas_call | solution.py:448
  52.3 1.6 %copy.11 = bf16[384,192]{0,1:T(8,128)(2,1)} copy(bf16[384,192]{0,1:T(8,128)(2,1)} %bitcast.4) | data formatting | bytes 294912

commit v4 on v3

--- a/solution.py
+++ b/solution.py
@@ -239,7 +239,7 @@
     def send_keys(part):
         span_rows = rows // parts
         source = pl.ds(part * span_rows, span_rows)
-        for level in [0] + list(range(levels - 1, 0, -1)):
+        for level in range(levels - 1, -1, -1):
             count = padded_rows(rows, level) // parts
             if level == 0:
                 src = kvbuf.at[:, source]

time: 54.1 us -> 55.8 us (1.031)
  Pallas kernels: 52.3 us -> 54.1 us
    pallas_call x1, Pallas kernels: 52.3 us -> 54.1 us  [local(): pl.pallas_call(functools.partial(kernel, tile_count, group_count, slide_t...]
where the time goes in v4:
time: 55.8 us; the launch traced here: 55.7 us
  Pallas kernels  54.1 us (97%)
  local copies, waits for them, and re-layouts  1.59 us (3%)
    pallas_call x1, Pallas kernels, local(): pl.pallas_call(functools.partial(kernel, tile_count, group_count, slide_t...  54.1 us
    unnamed x1, local copies, waits for them, and re-layouts  1.59 us

profile of v4, /device:TPU:0, one launch (start us, length us, event | category | flops | bytes accessed | tf_op | source)
XLA Modules:
  0.0 55.7 jit_solution(3488430613593751596)
XLA Ops:
  0.0 54.1 %shard_map.91 = bf16[192,384]{1,0:T(8,128)(2,1)} custom-call(bf16[192,384]{1,0:T(8,128)(2,1)} %bitcast.5, f32[768]{0:T(1024)} %gain1_hbm.1, bf16[3,192,768]{2,1,0:T(8,128)(2,1)} %bitcast.3, bf16[192,768]{1,0:T(8,128)(2,1)} %wo_hbm.1, f32[768]{0:T(1024)} %gain2_hbm.1, bf16[768,768]{1,0:T(8,128)(2,1)} %w1_hbm.1, bf16[768,768]{1,0:T(8,128)(2,1)} %w2_hbm.1, ...), custom_call_target="tpu_custom_call" | custom-call | tf_op jit(solution)/shard_map/pallas_call | solution.py:448
  54.1 1.6 %copy.11 = bf16[384,192]{0,1:T(8,128)(2,1)} copy(bf16[384,192]{0,1:T(8,128)(2,1)} %bitcast.4) | data formatting | bytes 294912
